TPU v7x, 32 devices: a whole 2x2x4 slice. The times are simulated.
32 devices in a mesh: dish: 4 (over y, x), blk: 8 (over z, core).
Axes of the slice: x: 2, y: 2, z: 4, core: 2. Of those that a mesh axis runs over, the one named last changes fastest.
Arguments:
- sky_data: float32 [4, 2048, 32768], P('dish', 'blk'), may hold values from -6 to 6
- eigenmodes: float32 [2048, 64], replicated, may hold values from -0.125 to 0.125
- noise_power: float32 [64, 32768], P('blk'), may hold values from 0.1 to 10
Outputs:
- cleaned: bfloat16 [4, 2048, 32768], P('dish', 'blk')
- mode_signal: float32 [4, 64, 32768], P('dish', 'blk')
All inputs are finite; a program needn't handle non-finite values.
Results may differ from a plain program's by a relative error of at most 0.0028.
Values may be sent and summed in bfloat16 or wider, within the bound.
A program may use at most 192 MiB of HBM per device.

v0:
```python
import math

import jax
import jax.numpy as jnp
from jax import lax
from jax.sharding import PartitionSpec as P

highest = lax.Precision.HIGHEST


def dft_table(length):
    index = jnp.arange(length, dtype=jnp.int32)
    phase = (index[:, None] * index[None, :] % length).astype(jnp.float32) * (
        2.0 * math.pi / length
    )
    return (jnp.cos(phase), jnp.sin(phase))


def twist_table(rows_count, cols_count):
    total = rows_count * cols_count
    first = jnp.arange(rows_count, dtype=jnp.int32)
    second = jnp.arange(cols_count, dtype=jnp.int32)
    phase = (first[:, None] * second[None, :] % total).astype(jnp.float32) * (2.0 * math.pi / total)
    return (jnp.cos(phase), jnp.sin(phase))


def forward(series, tables):
    col_cos, col_sin, row_cos, row_sin, twist_cos, twist_sin = tables
    batch_count, length = series.shape
    grid = series.reshape(batch_count, length // 128, 128)
    inner_real = jnp.einsum("bqp,qk->bpk", grid, col_cos, precision=highest)
    inner_imag = -jnp.einsum("bqp,qk->bpk", grid, col_sin, precision=highest)
    turned_real = inner_real * twist_cos + inner_imag * twist_sin
    turned_imag = inner_imag * twist_cos - inner_real * twist_sin
    spec_real = jnp.einsum("kp,bpj->bkj", row_cos, turned_real, precision=highest) + jnp.einsum(
        "kp,bpj->bkj", row_sin, turned_imag, precision=highest
    )
    spec_imag = jnp.einsum("kp,bpj->bkj", row_cos, turned_imag, precision=highest) - jnp.einsum(
        "kp,bpj->bkj", row_sin, turned_real, precision=highest
    )
    return (spec_real, spec_imag)


def inverse(held_real, held_imag, tables, length):
    col_cos, col_sin, row_cos, row_sin, twist_cos, twist_sin = tables
    outer_real = jnp.einsum("pk,bkj->bpj", row_cos, held_real, precision=highest) - jnp.einsum(
        "pk,bkj->bpj", row_sin, held_imag, precision=highest
    )
    outer_imag = jnp.einsum("pk,bkj->bpj", row_cos, held_imag, precision=highest) + jnp.einsum(
        "pk,bkj->bpj", row_sin, held_real, precision=highest
    )
    back_real = outer_real * twist_cos - outer_imag * twist_sin
    back_imag = outer_real * twist_sin + outer_imag * twist_cos
    series = jnp.einsum("qk,bpk->bqp", col_cos, back_real, precision=highest) - jnp.einsum(
        "qk,bpk->bqp", col_sin, back_imag, precision=highest
    )
    return (series / length).reshape(held_real.shape[0], length)


def wiener(amplitude, noise_power):
    dish_local = amplitude.shape[0]
    owned_modes = amplitude.shape[1]
    length = amplitude.shape[2]
    columns = length // 128
    col_cos, col_sin = dft_table(columns)
    row_cos, row_sin = dft_table(128)
    twist_cos, twist_sin = twist_table(128, columns)
    tables = (col_cos, col_sin, row_cos, row_sin, twist_cos, twist_sin)
    spec_real, spec_imag = forward(amplitude.reshape(dish_local * owned_modes, length), tables)
    squared = spec_real * spec_real + spec_imag * spec_imag
    power_here = jnp.sum(squared.reshape(dish_local, owned_modes, 128, columns), axis=0)
    power_total = lax.psum(power_here.astype(jnp.bfloat16), "dish").astype(jnp.float32)
    power = power_total / float(dish_local * lax.axis_size("dish") * length)
    gain = power / (power + noise_power.reshape(owned_modes, 128, columns))
    gain_rows = gain[None].reshape(dish_local * owned_modes, 128, columns)
    signal = inverse(spec_real * gain_rows, spec_imag * gain_rows, tables, length)
    return signal.reshape(dish_local, owned_modes, length)


def body(sky_data, eigenmodes, noise_power):
    channels = sky_data.shape[1]
    position = lax.axis_index("blk")
    local_modes = lax.dynamic_slice_in_dim(eigenmodes, position * channels, channels, 0)
    picked = local_modes
    summed = lax.psum_scatter(
        jnp.einsum("cm,dct->mdt", picked, sky_data, precision=highest),
        "blk",
        scatter_dimension=0,
        tiled=True,
    )
    owned_amplitude = jnp.transpose(summed, (1, 0, 2))
    signal = wiener(owned_amplitude, noise_power)
    picked = local_modes
    fitted = jnp.einsum(
        "cm,dmt->dct", picked, lax.all_gather(signal, "blk", axis=1, tiled=True), precision=highest
    )
    cleaned = (sky_data - fitted).astype(jnp.bfloat16)
    return (cleaned, signal)


def solution(mesh):
    return jax.shard_map(
        body,
        mesh=mesh,
        in_specs=(P("dish", "blk", None), P(), P("blk", None)),
        out_specs=(P("dish", "blk", None), P("dish", "blk", None)),
        check_vma=False,
    )
```

profile of v0, /device:TPU:0, one launch (start us, length us, event | category | flops | bytes accessed | tf_op | source)
XLA Modules:
  0.0 345.9 jit_solution(4713961836332405157)
XLA Ops:
  7.2 0.0 copy-start
  7.2 0.0 reduce-scatter.2.cloned.1.call-start
  7.2 1.0 copy-done
  8.2 25.2 %convolution_bitcast_fusion.1 = f32[64,1,32768]{2,0,1:T(8,128)} fusion(f32[1,256,32768]{2,1,0:T(8,128)} %param.3, f32[2048,64]{0,1:T(8,128)S(1)} %copy-done, s32[]{:T(128)S(6)} %select_n.63), kind=kOutput, calls=%fused_computation.3 | convolution fusion | flops 6442450944 | bytes 42008580 | tf_op jit(solution)/shard_map/cm,dct->mdt/dot_general | solution.py:86
  33.5 0.0 reduce-scatter.2.cloned.1.call-update
  33.5 0.2 all-reduce.2.cloned.1.call-start
  33.7 0.5 fusion.65
  34.2 91.7 %reduce-scatter.2.cloned.1.call-done = f32[8,1,32768]{2,0,1:T(8,128)} async-done(((f32[64,1,32768]{2,0,1:T(8,128)}), f32[8,1,32768]{2,0,1:T(8,128)}) %reduce-scatter.2.cloned.1.call-update) | async-done | bytes 1048592 | tf_op jit(solution)/shard_map/reduce_scatter | solution.py:85
  126.0 1.6 copy.17
  127.5 2.0 convolution_negate_fusion
  129.5 2.0 fusion.33
  131.5 2.0 fusion.39
  133.5 2.0 fusion.38
  135.6 2.0 fusion.7
  137.6 3.4 add_convert_fusion
  141.1 0.0 all-reduce.2.cloned.1.call-update
  141.1 0.0 all-gather.2.cloned.1.call-start
  141.1 1.6 copy.41
  142.7 1.3 copy.23
  144.0 40.9 %all-reduce.2.cloned.1.call-done = bf16[8,128,256]{1,2,0:T(8,128)(2,1)} async-done(((bf16[8,128,256]{1,2,0:T(8,128)(2,1)}), bf16[8,128,256]{1,2,0:T(8,128)(2,1)}) %all-reduce.2.cloned.1.call-update) | async-done | bytes 524304 | tf_op jit(solution)/shard_map/psum | solution.py:72
  184.9 2.9 fusion.25
  187.8 3.2 fusion.21
  191.0 2.9 fusion.4
  193.9 3.2 fusion.5
  197.1 2.0 fusion.13
  199.1 2.0 fusion.9
  201.1 0.3 copy.28
  201.5 1.2 reshape_reshape.3
  202.6 0.0 all-gather.2.cloned.1.call-update
  202.7 34.0 %copy.29 = f32[1,256,32768]{1,2,0:T(8,128)} copy(f32[1,256,32768]{2,1,0:T(8,128)} %param.3) | data formatting | bytes 67108864 | tf_op args[0]
  236.6 48.3 %all-gather.2.cloned.1.call-done = f32[1,64,32768]{2,1,0:T(8,128)} async-done(((f32[1,8,32768]{2,1,0:T(8,128)}), f32[1,64,32768]{2,1,0:T(8,128)}) %all-gather.2.cloned.1.call-update) | async-done | bytes 8388624 | tf_op jit(solution)/shard_map/all_gather | solution.py:95
  284.9 32.9 %fusion.1 = bf16[1,256,32768]{1,2,0:T(8,128)(2,1)} fusion(f32[1,256,32768]{1,2,0:T(8,128)} %copy.29, f32[1,64,32768]{2,1,0:T(8,128)} %all-gather.2.cloned.1.call-done, f32[2048,64]{0,1:T(8,128)S(1)} %copy-done, s32[]{:T(128)S(6)} %select_n.63), kind=kOutput, calls=%fused_computation.2 | convolution fusion | flops 6459228160 | bytes 58785796 | tf_op jit(solution)/shard_map/cm,dmt->dct/dot_general | solution.py:94
  317.8 21.2 %copy.30 = bf16[1,256,32768]{2,1,0:T(8,128)(2,1)} copy(bf16[1,256,32768]{1,2,0:T(8,128)(2,1)} %fusion.1) | data formatting | bytes 33554432
Async XLA Ops:
  7.2 1.0 copy-start
  7.2 118.8 %reduce-scatter.2.cloned.1.call-start = ((), (), s32[]{:S(2)}) async-start(), calls=%async_computation.1 | async-start | bytes 9437184 | tf_op jit(solution)/shard_map/reduce_scatter | solution.py:85
  33.5 151.4 %all-reduce.2.cloned.1.call-start = ((), (), s32[]{:S(2)}) async-start(), calls=%async_computation.2 | async-start | bytes 1048576 | tf_op jit(solution)/shard_map/psum | solution.py:72
  141.1 143.8 %all-gather.2.cloned.1.call-start = ((), (), s32[]{:S(2)}) async-start(), calls=%async_computation.3 | async-start | bytes 9437184 | tf_op jit(solution)/shard_map/all_gather | solution.py:95
Sparse Core Ops, SparseCore 0:
  33.6 92.3 reduce-scatter.1
  141.2 43.6 all-reduce.1
  202.8 82.0 all-gather.1
where the time goes:
time: 351 us; the launch traced here: 346 us
  waiting for transfers between devices  181 us (52%)
  matrix products  87.8 us (25%)
  local copies, waits for them, and re-layouts  62.1 us (18%)
  between operations  14.3 us (4%)
    reduce_scatter x1, waiting for transfers between devices, body(): lax.psum_scatter(jnp.einsum('cm,dct->mdt', picked, sky_data, precision=hi...  91.7 us
    unnamed x5, local copies, waits for them, and re-layouts  57.7 us
    all_gather x1, waiting for transfers between devices, body(): lax.all_gather(signal, 'blk', axis=1, tiled=True)  48.3 us
    psum x1, waiting for transfers between devices, wiener(): lax.psum(power_here.astype(jnp.bfloat16), 'dish').astype(jnp.float32)  40.9 us
    dot_general x1, matrix products, body(): jnp.einsum('cm,dmt->dct', picked, lax.all_gather(signal, 'blk', axis=1, t...  32.9 us
    dot_general x1, matrix products, body(): jnp.einsum('cm,dct->mdt', picked, sky_data, precision=highest)  25.2 us
  transfers between devices with their start and end apart: 3, of which 3 were waited for; matrix products, arithmetic and copies ran while one was open for 11% of the time, Pallas kernels for 0%

commit v1 on v0

--- a/solution.py
+++ b/solution.py
@@ -3,9 +3,11 @@
 import jax
 import jax.numpy as jnp
 from jax import lax
+from jax.experimental import pallas as pl
+from jax.experimental.pallas import tpu as pltpu
 from jax.sharding import PartitionSpec as P
 
-highest = lax.Precision.HIGHEST
+highest = lax.Precision.HIGH
 
 
 def dft_table(length):
@@ -77,24 +79,63 @@
     return signal.reshape(dish_local, owned_modes, length)
 
 
+def split(value):
+    top = value.astype(jnp.bfloat16)
+    return top, (value - top.astype(jnp.float32)).astype(jnp.bfloat16)
+
+
+def project_kernel(modes_ref, sky_ref, out_ref):
+    count = out_ref.shape[0]
+    top, rest = split(sky_ref[0])
+    both = jnp.dot(modes_ref[...], top, preferred_element_type=jnp.float32)
+    low = jnp.dot(modes_ref[:count], rest, preferred_element_type=jnp.float32)
+    out_ref[...] = (both[:count] + both[count:] + low).astype(out_ref.dtype)
+
+
+def clean_kernel(modes_ref, sky_ref, signal_ref, out_ref):
+    signal = signal_ref[...]
+    fitted = jnp.dot(
+        modes_ref[...],
+        jnp.concatenate([signal, signal], axis=0),
+        preferred_element_type=jnp.float32,
+    )
+    out_ref[0] = (sky_ref[0] - fitted).astype(jnp.bfloat16)
+
+
 def body(sky_data, eigenmodes, noise_power):
-    channels = sky_data.shape[1]
+    channels, length = sky_data.shape[1:]
+    count = eigenmodes.shape[1]
+    width = min(2048, length)
     position = lax.axis_index("blk")
     local_modes = lax.dynamic_slice_in_dim(eigenmodes, position * channels, channels, 0)
-    picked = local_modes
-    summed = lax.psum_scatter(
-        jnp.einsum("cm,dct->mdt", picked, sky_data, precision=highest),
-        "blk",
-        scatter_dimension=0,
-        tiled=True,
-    )
-    owned_amplitude = jnp.transpose(summed, (1, 0, 2))
-    signal = wiener(owned_amplitude, noise_power)
-    picked = local_modes
-    fitted = jnp.einsum(
-        "cm,dmt->dct", picked, lax.all_gather(signal, "blk", axis=1, tiled=True), precision=highest
-    )
-    cleaned = (sky_data - fitted).astype(jnp.bfloat16)
+    top, rest = split(local_modes)
+    wide = jnp.concatenate([top, rest], axis=1)
+    partial = pl.pallas_call(
+        project_kernel,
+        grid=(length // width,),
+        in_specs=[
+            pl.BlockSpec((2 * count, channels), lambda i: (0, 0)),
+            pl.BlockSpec((1, channels, width), lambda i: (0, 0, i)),
+        ],
+        out_specs=pl.BlockSpec((count, width), lambda i: (0, i)),
+        out_shape=jax.ShapeDtypeStruct((count, length), jnp.float32),
+        compiler_params=pltpu.CompilerParams(vmem_limit_bytes=40 * 2**20),
+    )(wide.T, sky_data)
+    summed = lax.psum_scatter(partial, "blk", scatter_dimension=0, tiled=True)
+    signal = wiener(summed[None], noise_power)
+    everyone = lax.all_gather(signal[0].astype(jnp.bfloat16), "blk", axis=0, tiled=True)
+    cleaned = pl.pallas_call(
+        clean_kernel,
+        grid=(length // width,),
+        in_specs=[
+            pl.BlockSpec((channels, 2 * count), lambda i: (0, 0)),
+            pl.BlockSpec((1, channels, width), lambda i: (0, 0, i)),
+            pl.BlockSpec((count, width), lambda i: (0, i)),
+        ],
+        out_specs=pl.BlockSpec((1, channels, width), lambda i: (0, 0, i)),
+        out_shape=jax.ShapeDtypeStruct(sky_data.shape, jnp.bfloat16),
+        compiler_params=pltpu.CompilerParams(vmem_limit_bytes=40 * 2**20),
+    )(wide, sky_data, everyone)
     return (cleaned, signal)
 
 

time: 351 us -> 273 us (0.78); the launches traced: 346 us -> 272 us
  matrix products: 87.8 us -> 22.6 us
  local copies, waits for them, and re-layouts: 62.1 us -> 13.8 us
  Pallas kernels: 0 us -> 42.2 us
    dot_general x2 -> x0, matrix products: 58.1 us -> none  [the longest x1 32.9 us: body(): jnp.einsum('cm,dmt->dct', picked, lax.all_gather(signal, 'blk', axis=1, t...]
    unnamed x5 -> x10, local copies, waits for them, and re-layouts: 57.7 us -> 8.24 us
    pallas_call x0 -> x2, Pallas kernels: none -> 42.2 us  [the longest x1 23.4 us: body(): pl.pallas_call(clean_kernel, grid=(length // width,), in_specs=[pl.BlockS...]
  transfers between devices with their start and end apart: 3 -> 3, of which waited for: 3 -> 3; matrix products, arithmetic and copies ran while one was open for 11% -> 2% of each run, Pallas kernels for 0% -> 0%
where the time goes in v1:
time: 273 us; the launch traced here: 272 us
  waiting for transfers between devices  178 us (65%)
  Pallas kernels  42.2 us (15%)
  matrix products  22.6 us (8%)
  between operations  13.9 us (5%)
  local copies, waits for them, and re-layouts  13.8 us (5%)
    reduce_scatter x1, waiting for transfers between devices, body(): summed = lax.psum_scatter(partial, 'blk', scatter_dimension=0, tiled=True)  91.9 us
    all_gather x1, waiting for transfers between devices, body(): lax.all_gather(signal[0].astype(jnp.bfloat16), 'blk', axis=0, tiled=True)  45.7 us
    psum x1, waiting for transfers between devices, wiener(): lax.psum(power_here.astype(jnp.bfloat16), 'dish').astype(jnp.float32)  40.7 us
    pallas_call x1, Pallas kernels, body(): pl.pallas_call(clean_kernel, grid=(length // width,), in_specs=[pl.BlockS...  23.4 us
    pallas_call x1, Pallas kernels, body(): pl.pallas_call(project_kernel, grid=(length // width,), in_specs=[pl.Bloc...  18.8 us
    unnamed x10, local copies, waits for them, and re-layouts  8.24 us
  transfers between devices with their start and end apart: 3, of which 3 were waited for; matrix products, arithmetic and copies ran while one was open for 2% of the time, Pallas kernels for 0%

profile of v1, /device:TPU:0, one launch (start us, length us, event | category | flops | bytes accessed | tf_op | source)
XLA Modules:
  0.0 271.8 jit_solution(3175974703652567931)
XLA Ops:
  7.2 0.0 copy-start
  7.2 0.0 reduce-scatter.2.cloned.1.call-start
  7.2 1.0 copy-done
  8.2 0.1 copy.41
  8.3 0.1 fusion.125
  8.4 0.1 copy.19.modes_ref
  8.6 18.8 %shard_map.50 = f32[64,32768]{1,0:T(8,128)S(1)} custom-call(bf16[128,256]{1,0:T(8,128)(2,1)S(1)} %copy.19.modes_ref, f32[1,256,32768]{2,1,0:T(8,128)} %sky_ref.3), custom_call_target="tpu_custom_call" | custom-call | tf_op jit(solution)/shard_map/pallas_call | solution.py:113
  27.3 0.0 copy-start.2
  27.3 3.4 %copy-done.2 = f32[64,32768]{1,0:T(8,128)} copy-done((f32[64,32768]{1,0:T(8,128)}, f32[64,32768]{1,0:T(8,128)S(1)}, u32[]{:S(2)}) %copy-start.2) | copy-done | bytes 8388632
  30.7 0.0 reduce-scatter.2.cloned.1.call-update
  30.7 0.0 all-reduce.2.cloned.1.call-start
  30.8 0.5 fusion.61
  31.3 91.9 %reduce-scatter.2.cloned.1.call-done = f32[8,32768]{1,0:T(8,128)} async-done(((f32[64,32768]{1,0:T(8,128)}), f32[8,32768]{1,0:T(8,128)}) %reduce-scatter.2.cloned.1.call-update) | async-done | bytes 1048592 | tf_op jit(solution)/shard_map/reduce_scatter | solution.py:124
  123.2 1.6 copy.20
  124.8 1.6 convolution_negate_fusion
  126.3 1.5 fusion.29
  127.9 1.2 fusion.35
  129.1 1.2 fusion.34
  130.3 1.2 fusion.3
  131.6 2.4 add_convert_fusion
  134.0 0.0 all-reduce.2.cloned.1.call-update
  134.0 0.2 all-gather.2.cloned.1.call-start
  134.3 1.6 copy.44
  135.8 1.3 copy.26
  137.1 40.7 %all-reduce.2.cloned.1.call-done = bf16[8,128,256]{1,2,0:T(8,128)(2,1)} async-done(((bf16[8,128,256]{1,2,0:T(8,128)(2,1)}), bf16[8,128,256]{1,2,0:T(8,128)(2,1)}) %all-reduce.2.cloned.1.call-update) | async-done | bytes 524304 | tf_op jit(solution)/shard_map/psum | solution.py:74
  177.9 2.4 fusion.21
  180.2 2.7 fusion.17
  182.9 2.4 fusion
  185.3 2.7 fusion.1
  188.0 1.6 fusion.9
  189.7 1.6 fusion.122
  191.3 1.1 copy.31
  192.4 0.0 all-gather.2.cloned.1.call-update
  192.4 0.1 pad_maximum_fusion.modes_ref
  192.5 0.3 copy.32
  192.9 0.0 copy-start.1
  192.9 1.2 reshape_reshape.3
  194.0 45.7 %all-gather.2.cloned.1.call-done.signal_ref = bf16[64,32768]{1,0:T(8,128)(2,1)} async-done(((bf16[8,32768]{1,0:T(8,128)(2,1)}), bf16[64,32768]{1,0:T(8,128)(2,1)}) %all-gather.2.cloned.1.call-update) | async-done | bytes 4194320 | tf_op jit(solution)/shard_map/all_gather | solution.py:126
  239.7 0.0 copy-start.3
  239.7 2.2 copy-done.3
  241.9 23.4 %shard_map.51 = bf16[1,256,32768]{2,1,0:T(8,128)(2,1)} custom-call(bf16[256,128]{1,0:T(8,128)(2,1)S(1)} %pad_maximum_fusion.modes_ref, f32[1,256,32768]{2,1,0:T(8,128)} %sky_ref.3, bf16[64,32768]{1,0:T(8,128)(2,1)S(1)} %copy-done.3), custom_call_target="tpu_custom_call" | custom-call | tf_op jit(solution)/shard_map/pallas_call | solution.py:127
  265.3 0.0 copy-done.1
  (2 shorter events, 0.0 us)
Async XLA Ops:
  7.2 1.1 copy-start
  7.2 116.0 %reduce-scatter.2.cloned.1.call-start = ((), (), s32[]{:S(2)}) async-start(), calls=%async_computation.1 | async-start | bytes 9437184 | tf_op jit(solution)/shard_map/reduce_scatter | solution.py:124
  27.3 3.4 %copy-start.2 = (f32[64,32768]{1,0:T(8,128)}, f32[64,32768]{1,0:T(8,128)S(1)}, u32[]{:S(2)}) copy-start(f32[64,32768]{1,0:T(8,128)S(1)} %shard_map.50) | copy-start | bytes 25165828
  30.7 147.1 %all-reduce.2.cloned.1.call-start = ((), (), s32[]{:S(2)}) async-start(), calls=%async_computation.2 | async-start | bytes 1048576 | tf_op jit(solution)/shard_map/psum | solution.py:74
  134.0 105.7 %all-gather.2.cloned.1.call-start = ((), (), s32[]{:S(2)}) async-start(), calls=%async_computation.3 | async-start | bytes 4718592 | tf_op jit(solution)/shard_map/all_gather | solution.py:126
  192.9 72.4 %copy-start.1 = (f32[2048,64]{0,1:T(8,128)S(1)}, f32[2048,64]{0,1:T(8,128)}, u32[]{:S(2)}) copy-start(f32[2048,64]{0,1:T(8,128)} %param.4) | copy-start | bytes 1572868
  239.7 2.2 copy-start.3
Sparse Core Ops, SparseCore 0:
  30.9 92.2 reduce-scatter.1
  134.1 43.6 all-reduce.1
  192.6 47.1 all-gather.1

commit v2 on v1

--- a/solution.py
+++ b/solution.py
@@ -1,3 +1,4 @@
+import functools
 import math
 
 import jax
@@ -71,7 +72,7 @@
     spec_real, spec_imag = forward(amplitude.reshape(dish_local * owned_modes, length), tables)
     squared = spec_real * spec_real + spec_imag * spec_imag
     power_here = jnp.sum(squared.reshape(dish_local, owned_modes, 128, columns), axis=0)
-    power_total = lax.psum(power_here.astype(jnp.bfloat16), "dish").astype(jnp.float32)
+    power_total = sum_over_dishes(power_here)
     power = power_total / float(dish_local * lax.axis_size("dish") * length)
     gain = power / (power + noise_power.reshape(owned_modes, 128, columns))
     gain_rows = gain[None].reshape(dish_local * owned_modes, 128, columns)
@@ -84,12 +85,250 @@
     return top, (value - top.astype(jnp.float32)).astype(jnp.bfloat16)
 
 
-def project_kernel(modes_ref, sky_ref, out_ref):
-    count = out_ref.shape[0]
-    top, rest = split(sky_ref[0])
-    both = jnp.dot(modes_ref[...], top, preferred_element_type=jnp.float32)
-    low = jnp.dot(modes_ref[:count], rest, preferred_element_type=jnp.float32)
-    out_ref[...] = (both[:count] + both[count:] + low).astype(out_ref.dtype)
+MESH = pl.DeviceIdType.MESH
+
+
+def scatter_kernel(
+    chips, chunks, wire, modes_ref, sky_ref, out_ref,
+    own, give, taken, stage_up, stage_down, from_below, from_above,
+    pair_send, pair_recv, up_send, up_recv, down_send, down_recv,
+):
+    step = pl.program_id(0)
+    me = lax.axis_index("blk")
+    place = me // 2
+    partner = me + 1 - 2 * (me % 2)
+    has_below = place > 0
+    has_above = place < chips - 1
+    half = modes_ref.shape[0] // 4
+    count = half // chips
+    folded = out_ref.shape[2]
+    folds = out_ref.shape[1] // count
+
+    def pair_copy(chunk):
+        return pltpu.make_async_remote_copy(
+            src_ref=give.at[chunk], dst_ref=taken.at[chunk],
+            send_sem=pair_send.at[chunk], recv_sem=pair_recv.at[chunk],
+            device_id={"blk": partner}, device_id_type=MESH,
+        )
+
+    def up_copy(chunk, target):
+        return pltpu.make_async_remote_copy(
+            src_ref=stage_up.at[chunk, target], dst_ref=from_below.at[chunk, target],
+            send_sem=up_send.at[chunk, target], recv_sem=up_recv.at[chunk, target],
+            device_id={"blk": me + 2}, device_id_type=MESH,
+        )
+
+    def down_copy(chunk, target):
+        return pltpu.make_async_remote_copy(
+            src_ref=stage_down.at[chunk, target], dst_ref=from_above.at[chunk, target],
+            send_sem=down_send.at[chunk, target], recv_sem=down_recv.at[chunk, target],
+            device_id={"blk": me - 2}, device_id_type=MESH,
+        )
+
+    @pl.when(step == 0)
+    def _():
+        barrier = pltpu.get_barrier_semaphore()
+        pl.semaphore_signal(barrier, inc=1, device_id={"blk": partner}, device_id_type=MESH)
+
+        @pl.when(has_below)
+        def _():
+            pl.semaphore_signal(barrier, inc=1, device_id={"blk": me - 2}, device_id_type=MESH)
+
+        @pl.when(has_above)
+        def _():
+            pl.semaphore_signal(barrier, inc=1, device_id={"blk": me + 2}, device_id_type=MESH)
+
+        pl.semaphore_wait(
+            barrier, 1 + jnp.where(has_below, 1, 0) + jnp.where(has_above, 1, 0)
+        )
+
+    @pl.when(step < chunks)
+    def _():
+        top, rest = split(sky_ref[0])
+        both = jnp.dot(modes_ref[...], top, preferred_element_type=jnp.float32)
+        low = jnp.dot(modes_ref[: 2 * half], rest, preferred_element_type=jnp.float32)
+        share = both[: 2 * half] + both[2 * half :] + low
+        for target in range(chips):
+            for buffer, start in ((own, target * count), (give, half + target * count)):
+                buffer[step, target] = jnp.concatenate(
+                    [
+                        share[start : start + count, fold * folded : (fold + 1) * folded]
+                        for fold in range(folds)
+                    ],
+                    axis=0,
+                )
+        pair_copy(step).start()
+
+    paired = step - 1
+
+    @pl.when((paired >= 0) & (paired < chunks))
+    def _():
+        pair_copy(paired).wait_recv()
+        own[paired] += taken[paired]
+
+    rising = step - 1 - place
+
+    @pl.when((rising >= 0) & (rising < chunks))
+    def _():
+        for target in range(chips - 1, -1, -1):
+            @pl.when(has_below & (target >= place))
+            def _():
+                up_copy(rising, target).wait_recv()
+
+            @pl.when(has_below & (target > place))
+            def _():
+                stage_up[rising, target] = (
+                    own[rising, target] + from_below[rising, target].astype(jnp.float32)
+                ).astype(wire)
+
+            @pl.when((place == 0) & (target > place))
+            def _():
+                stage_up[rising, target] = own[rising, target].astype(wire)
+
+            @pl.when(target > place)
+            def _():
+                up_copy(rising, target).start()
+
+    falling = step - chips + place
+
+    @pl.when((falling >= 0) & (falling < chunks))
+    def _():
+        for target in range(chips):
+            @pl.when(has_above & (target <= place))
+            def _():
+                down_copy(falling, target).wait_recv()
+
+            @pl.when(has_above & (target < place))
+            def _():
+                stage_down[falling, target] = (
+                    own[falling, target] + from_above[falling, target].astype(jnp.float32)
+                ).astype(wire)
+
+            @pl.when((place == chips - 1) & (target < place))
+            def _():
+                stage_down[falling, target] = own[falling, target].astype(wire)
+
+            @pl.when(target < place)
+            def _():
+                down_copy(falling, target).start()
+
+    ready = step - 1 - jnp.maximum(place, chips - 1 - place)
+
+    @pl.when((ready >= 0) & (ready < chunks))
+    def _():
+        out_ref[ready] = own[ready, place]
+
+        @pl.when(has_below)
+        def _():
+            out_ref[ready] += from_below[ready, place].astype(jnp.float32)
+
+        @pl.when(has_above)
+        def _():
+            out_ref[ready] += from_above[ready, place].astype(jnp.float32)
+
+    @pl.when(step == chunks + chips - 1)
+    def _():
+        def drain(chunk, carry):
+            pair_copy(chunk).wait_send()
+            for target in range(chips):
+                @pl.when(target > place)
+                def _():
+                    up_copy(chunk, target).wait_send()
+
+                @pl.when(target < place)
+                def _():
+                    down_copy(chunk, target).wait_send()
+
+            return carry
+
+        lax.fori_loop(0, chunks, drain, 0)
+
+
+def project(sky_data, local_modes):
+    channels, length = sky_data.shape[1:]
+    modes = local_modes.shape[1]
+    chips = lax.axis_size("blk") // 2
+    count = modes // (2 * chips)
+    folds = max(16 // count, 1)
+    width = 2048
+    chunks = length // width
+    core = lax.axis_index("blk") % 2
+    by_core = local_modes.reshape(channels, chips, 2, count)
+    mine = lax.dynamic_index_in_dim(by_core, core, 2, keepdims=False)
+    others = lax.dynamic_index_in_dim(by_core, 1 - core, 2, keepdims=False)
+    ordered = jnp.concatenate([mine.reshape(channels, -1), others.reshape(channels, -1)], axis=1)
+    wide = jnp.concatenate(split(ordered), axis=1).T
+    wire = jnp.bfloat16 if chips <= 4 else jnp.float32
+    block = (chunks, chips, folds * count, width // folds)
+    summed = pl.pallas_call(
+        functools.partial(scatter_kernel, chips, chunks, wire),
+        grid=(chunks + chips,),
+        in_specs=[
+            pl.BlockSpec(wide.shape, lambda i: (0, 0)),
+            pl.BlockSpec((1, channels, width), lambda i: (0, 0, jnp.minimum(i, chunks - 1))),
+        ],
+        out_specs=pl.BlockSpec((chunks,) + block[2:], lambda i: (0, 0, 0)),
+        out_shape=jax.ShapeDtypeStruct((chunks,) + block[2:], jnp.float32),
+        scratch_shapes=[pltpu.VMEM(block, jnp.float32)] * 3
+        + [pltpu.VMEM(block, wire)] * 4
+        + [pltpu.SemaphoreType.DMA((chunks,))] * 2
+        + [pltpu.SemaphoreType.DMA((chunks, chips))] * 4,
+        compiler_params=pltpu.CompilerParams(
+            collective_id=0, has_side_effects=True, vmem_limit_bytes=56 * 2**20
+        ),
+    )(wide, sky_data)
+    summed = summed.reshape(chunks, folds, count, width // folds)
+    return jnp.transpose(summed, (2, 0, 1, 3)).reshape(count, length)
+
+
+def power_kernel(rounds, here_ref, out_ref, stage, taken, send, recv):
+    me = lax.axis_index("dish")
+    middle = here_ref.shape[1] // 2
+
+    def peer(bit):
+        return me + (1 << bit) - 2 * ((me // (1 << bit)) % 2) * (1 << bit)
+
+    barrier = pltpu.get_barrier_semaphore()
+    for bit in range(rounds):
+        pl.semaphore_signal(barrier, inc=1, device_id={"dish": peer(bit)}, device_id_type=MESH)
+    pl.semaphore_wait(barrier, rounds)
+    out_ref[...] = here_ref[...]
+    for turn in range(rounds):
+        copies = []
+        for side in range(2):
+            bit = turn if side == 0 else rounds - 1 - turn
+            rows = pl.ds(side * middle, middle)
+            stage[turn, side] = out_ref[:, rows, :].astype(stage.dtype)
+            copy = pltpu.make_async_remote_copy(
+                src_ref=stage.at[turn, side], dst_ref=taken.at[turn, side],
+                send_sem=send.at[turn, side], recv_sem=recv.at[turn, side],
+                device_id={"dish": peer(bit)}, device_id_type=MESH,
+            )
+            copy.start()
+            copies.append((copy, rows))
+        for side, (copy, rows) in enumerate(copies):
+            copy.wait()
+            out_ref[:, rows, :] += taken[turn, side].astype(jnp.float32)
+
+
+def sum_over_dishes(power_here):
+    dishes = lax.axis_size("dish")
+    rounds = dishes.bit_length() - 1
+    if rounds == 0 or dishes != 1 << rounds:
+        return lax.psum(power_here, "dish")
+    count, rows, columns = power_here.shape
+    half = (rounds, 2, count, rows // 2, columns)
+    return pl.pallas_call(
+        functools.partial(power_kernel, rounds),
+        in_specs=[pl.BlockSpec(memory_space=pltpu.VMEM)],
+        out_specs=pl.BlockSpec(memory_space=pltpu.VMEM),
+        out_shape=jax.ShapeDtypeStruct(power_here.shape, jnp.float32),
+        scratch_shapes=[pltpu.VMEM(half, jnp.bfloat16)] * 2
+        + [pltpu.SemaphoreType.DMA((rounds, 2))] * 2,
+        compiler_params=pltpu.CompilerParams(
+            collective_id=1, has_side_effects=True, vmem_limit_bytes=32 * 2**20
+        ),
+    )(power_here)
 
 
 def clean_kernel(modes_ref, sky_ref, signal_ref, out_ref):
@@ -110,19 +349,7 @@
     local_modes = lax.dynamic_slice_in_dim(eigenmodes, position * channels, channels, 0)
     top, rest = split(local_modes)
     wide = jnp.concatenate([top, rest], axis=1)
-    partial = pl.pallas_call(
-        project_kernel,
-        grid=(length // width,),
-        in_specs=[
-            pl.BlockSpec((2 * count, channels), lambda i: (0, 0)),
-            pl.BlockSpec((1, channels, width), lambda i: (0, 0, i)),
-        ],
-        out_specs=pl.BlockSpec((count, width), lambda i: (0, i)),
-        out_shape=jax.ShapeDtypeStruct((count, length), jnp.float32),
-        compiler_params=pltpu.CompilerParams(vmem_limit_bytes=40 * 2**20),
-    )(wide.T, sky_data)
-    summed = lax.psum_scatter(partial, "blk", scatter_dimension=0, tiled=True)
-    signal = wiener(summed[None], noise_power)
+    signal = wiener(project(sky_data, local_modes)[None], noise_power)
     everyone = lax.all_gather(signal[0].astype(jnp.bfloat16), "blk", axis=0, tiled=True)
     cleaned = pl.pallas_call(
         clean_kernel,

time: 273 us -> 181 us (0.66)
  waiting for transfers between devices: 178 us -> 43.8 us
  Pallas kernels: 42.2 us -> 97.6 us
  matrix products: 22.6 us -> 14.3 us
  local copies, waits for them, and re-layouts: 13.8 us -> 8.81 us
    reduce_scatter x1 -> x0, waiting for transfers between devices: 91.9 us -> none  [body(): summed = lax.psum_scatter(partial, 'blk', scatter_dimension=0, tiled=True)]
    pallas_call x1 -> x2, Pallas kernels: 18.8 us -> 74.3 us  [the longest x1 59.9 us: project(): pl.pallas_call(functools.partial(scatter_kernel, chips, chunks, wire), gr...]
    psum x1 -> x0, waiting for transfers between devices: 40.7 us -> none  [wiener(): lax.psum(power_here.astype(jnp.bfloat16), 'dish').astype(jnp.float32)]
    unnamed x10 -> x9, local copies, waits for them, and re-layouts: 8.24 us -> 3.27 us
  transfers between devices with their start and end apart: 3 -> 1, of which waited for: 3 -> 1; matrix products, arithmetic and copies ran while one was open for 2% -> 1% of each run, Pallas kernels for 0% -> 0%
where the time goes in v2:
time: 181 us
  Pallas kernels  97.6 us (54%)
  waiting for transfers between devices  43.8 us (24%)
  matrix products  14.3 us (8%)
  between operations  14.2 us (8%)
  local copies, waits for them, and re-layouts  8.81 us (5%)
    pallas_call x1, Pallas kernels, project(): pl.pallas_call(functools.partial(scatter_kernel, chips, chunks, wire), gr...  59.9 us
    all_gather x1, waiting for transfers between devices, body(): lax.all_gather(signal[0].astype(jnp.bfloat16), 'blk', axis=0, tiled=True)  43.8 us
    pallas_call x1, Pallas kernels, body(): pl.pallas_call(clean_kernel, grid=(length // width,), in_specs=[pl.BlockS...  23.4 us
    pallas_call x1, Pallas kernels, sum_over_dishes(): pl.pallas_call(functools.partial(power_kernel, rounds), in_specs=[pl.Bloc...  14.4 us
  transfers between devices with their start and end apart: 1, of which 1 were waited for; matrix products, arithmetic and copies ran while one was open for 1% of the time, Pallas kernels for 0%

profile of v2, /device:TPU:0, one launch (start us, length us, event | category | flops | bytes accessed | tf_op | source)
XLA Modules:
  0.0 180.5 jit_solution(16944134828190532475)
XLA Ops:
  7.2 0.0 copy-start
  7.2 0.0 all-gather.2.cloned.1.call-start
  7.2 1.0 copy-done
  8.3 0.5 fusion.61
  8.8 0.6 maximum_bitcast_fusion.modes_ref
  9.4 59.9 %shard_map.50 = f32[16,16,1024]{2,1,0:T(8,128)} custom-call(bf16[128,256]{1,0:T(8,128)(2,1)} %maximum_bitcast_fusion.modes_ref, f32[1,256,32768]{2,1,0:T(8,128)} %sky_ref.3), custom_call_target="tpu_custom_call" | custom-call | tf_op jit(solution)/shard_map/pallas_call | solution.py:263
  69.3 0.0 copy-start.3
  69.3 2.1 %copy.68 = f32[16,2,8,1024]{3,1,0,2:T(2,128)S(1)} copy(f32[16,2,8,1024]{3,2,1,0:T(8,128)} %bitcast.59) | data formatting | bytes 2097152 | tf_op jit(solution)/shard_map/reshape | solution.py:280
  71.5 0.8 reshape_reshape_broadcast_in_dim_reshape.3
  72.3 1.9 %convolution_negate_fusion = f32[8,128,256]{2,1,0:T(8,128)S(1)} fusion(f32[8,256,128]{2,1,0:T(8,128)S(1)} %reshape_reshape_broadcast_in_dim_reshape.3), kind=kOutput, calls=%fused_computation.9 | convolution fusion | flops 403832832 | bytes 2097152 | tf_op jit(solution)/shard_map/bqp,qk->bpk/dot_general | solution.py:35
  74.2 1.8 %fusion.29 = f32[8,128,256]{2,1,0:T(8,128)S(1)} fusion(f32[8,256,128]{2,1,0:T(8,128)S(1)} %reshape_reshape_broadcast_in_dim_reshape.3), kind=kOutput, calls=%fused_computation.43 | convolution fusion | flops 403570688 | bytes 2097152 | tf_op jit(solution)/shard_map/bqp,qk->bpk/dot_general | solution.py:34
  76.0 0.9 fusion.35
  76.9 0.9 fusion.34
  77.8 0.9 fusion.3
  78.7 1.0 multiply_add_fusion
  79.7 14.4 %shard_map.51 = f32[8,128,256]{2,1,0:T(8,128)S(1)} custom-call(f32[8,128,256]{2,1,0:T(8,128)S(1)} %get-tuple-element.6.here_ref), custom_call_target="tpu_custom_call" | custom-call | tf_op jit(solution)/shard_map/pallas_call | solution.py:321
  94.1 0.0 copy-done.3
  94.1 0.4 add_divide_fusion
  94.5 0.8 fusion.21
  95.4 1.0 fusion.17
  96.4 0.9 fusion
  97.3 0.8 fusion.1
  98.1 1.6 fusion.9
  99.8 1.6 fusion.123
  101.4 1.1 copy.44
  102.5 0.0 all-gather.2.cloned.1.call-update
  102.5 0.1 copy.64
  102.6 0.3 copy.45
  103.0 1.2 reshape_reshape.3
  104.2 0.0 copy-start.1
  104.2 0.1 pad_maximum_fusion.modes_ref
  104.3 43.8 %all-gather.2.cloned.1.call-done.signal_ref = bf16[64,32768]{1,0:T(8,128)(2,1)} async-done(((bf16[8,32768]{1,0:T(8,128)(2,1)}), bf16[64,32768]{1,0:T(8,128)(2,1)}) %all-gather.2.cloned.1.call-update) | async-done | bytes 4194320 | tf_op jit(solution)/shard_map/all_gather | solution.py:353
  148.1 0.0 copy-start.2
  148.1 2.2 %copy-done.2 = bf16[64,32768]{1,0:T(8,128)(2,1)S(1)} copy-done((bf16[64,32768]{1,0:T(8,128)(2,1)S(1)}, bf16[64,32768]{1,0:T(8,128)(2,1)}, u32[]{:S(2)}) %copy-start.2) | copy-done | bytes 4194328
  150.3 23.4 %shard_map.52 = bf16[1,256,32768]{2,1,0:T(8,128)(2,1)} custom-call(bf16[256,128]{1,0:T(8,128)(2,1)S(1)} %pad_maximum_fusion.modes_ref, f32[1,256,32768]{2,1,0:T(8,128)} %sky_ref.3, bf16[64,32768]{1,0:T(8,128)(2,1)S(1)} %copy-done.2), custom_call_target="tpu_custom_call" | custom-call | tf_op jit(solution)/shard_map/pallas_call | solution.py:354
  173.7 0.0 copy-done.1
  (5 shorter events, 0.0 us)
Async XLA Ops:
  7.2 1.1 copy-start
  7.2 140.9 %all-gather.2.cloned.1.call-start = ((), (), s32[]{:S(2)}) async-start(), calls=%async_computation | async-start | bytes 4718592 | tf_op jit(solution)/shard_map/all_gather | solution.py:353
  69.3 24.8 %copy-start.3 = (f32[8,32768]{1,0:T(8,128)S(1)}, f32[8,32768]{1,0:T(8,128)}, u32[]{:S(2)}) copy-start(f32[8,32768]{1,0:T(8,128)} %param.5) | copy-start | bytes 3145732
  104.2 69.5 %copy-start.1 = (f32[2048,64]{0,1:T(8,128)S(1)}, f32[2048,64]{0,1:T(8,128)}, u32[]{:S(2)}) copy-start(f32[2048,64]{0,1:T(8,128)} %param.4) | copy-start | bytes 1572868
  148.1 2.2 %copy-start.2 = (bf16[64,32768]{1,0:T(8,128)(2,1)S(1)}, bf16[64,32768]{1,0:T(8,128)(2,1)}, u32[]{:S(2)}) copy-start(bf16[64,32768]{1,0:T(8,128)(2,1)} %all-gather.2.cloned.1.call-done.signal_ref) | copy-start | bytes 12582916
Sparse Core Ops, SparseCore 0:
  102.7 45.3 all-gather.1

commit v3 on v2

--- a/solution.py
+++ b/solution.py
@@ -85,7 +85,13 @@
     return top, (value - top.astype(jnp.float32)).astype(jnp.bfloat16)
 
 
+def split_rounded(value):
+    top = lax.reduce_precision(value, 8, 7)
+    return top.astype(jnp.bfloat16), (value - top).astype(jnp.bfloat16)
+
+
 MESH = pl.DeviceIdType.MESH
+AHEAD = 2
 
 
 def scatter_kernel(
@@ -170,6 +176,13 @@
 
     @pl.when((rising >= 0) & (rising < chunks))
     def _():
+        @pl.when(rising >= AHEAD)
+        def _():
+            for target in range(1, chips):
+                @pl.when(target > place)
+                def _():
+                    up_copy(rising - AHEAD, target).wait_send()
+
         for target in range(chips - 1, -1, -1):
             @pl.when(has_below & (target >= place))
             def _():
@@ -193,6 +206,13 @@
 
     @pl.when((falling >= 0) & (falling < chunks))
     def _():
+        @pl.when(falling >= AHEAD)
+        def _():
+            for target in range(chips - 1):
+                @pl.when(target < place)
+                def _():
+                    down_copy(falling - AHEAD, target).wait_send()
+
         for target in range(chips):
             @pl.when(has_above & (target <= place))
             def _():
@@ -230,6 +250,9 @@
     def _():
         def drain(chunk, carry):
             pair_copy(chunk).wait_send()
+            return carry
+
+        def drain_line(chunk, carry):
             for target in range(chips):
                 @pl.when(target > place)
                 def _():
@@ -242,6 +265,7 @@
             return carry
 
         lax.fori_loop(0, chunks, drain, 0)
+        lax.fori_loop(chunks - AHEAD, chunks, drain_line, 0)
 
 
 def project(sky_data, local_modes):
@@ -257,7 +281,7 @@
     mine = lax.dynamic_index_in_dim(by_core, core, 2, keepdims=False)
     others = lax.dynamic_index_in_dim(by_core, 1 - core, 2, keepdims=False)
     ordered = jnp.concatenate([mine.reshape(channels, -1), others.reshape(channels, -1)], axis=1)
-    wide = jnp.concatenate(split(ordered), axis=1).T
+    wide = jnp.concatenate(split_rounded(ordered), axis=1).T
     wire = jnp.bfloat16 if chips <= 4 else jnp.float32
     block = (chunks, chips, folds * count, width // folds)
     summed = pl.pallas_call(
@@ -331,38 +355,60 @@
     )(power_here)
 
 
-def clean_kernel(modes_ref, sky_ref, signal_ref, out_ref):
-    signal = signal_ref[...]
-    fitted = jnp.dot(
-        modes_ref[...],
-        jnp.concatenate([signal, signal], axis=0),
-        preferred_element_type=jnp.float32,
-    )
-    out_ref[0] = (sky_ref[0] - fitted).astype(jnp.bfloat16)
-
-
-def body(sky_data, eigenmodes, noise_power):
-    channels, length = sky_data.shape[1:]
-    count = eigenmodes.shape[1]
-    width = min(2048, length)
-    position = lax.axis_index("blk")
-    local_modes = lax.dynamic_slice_in_dim(eigenmodes, position * channels, channels, 0)
-    top, rest = split(local_modes)
-    wide = jnp.concatenate([top, rest], axis=1)
-    signal = wiener(project(sky_data, local_modes)[None], noise_power)
-    everyone = lax.all_gather(signal[0].astype(jnp.bfloat16), "blk", axis=0, tiled=True)
-    cleaned = pl.pallas_call(
+def clean_kernel(modes_ref, sky_ref, signal_ref, *rest):
+    out_ref = rest[-1]
+    tile = 256
+    for start in range(0, out_ref.shape[2], tile):
+        columns = slice(start, start + tile)
+        signal = signal_ref[:, columns]
+        fitted = jnp.dot(
+            modes_ref[...],
+            jnp.concatenate([signal, signal], axis=0),
+            preferred_element_type=jnp.float32,
+        )
+        out_ref[0, :, columns] = (sky_ref[0, :, columns] - fitted).astype(jnp.bfloat16)
+
+
+def clean(sky_data, wide, signal, first, before):
+    channels = sky_data.shape[1]
+    count, length = signal.shape
+    width = 2048
+    skip = first // width
+    held = [] if before is None else [before]
+    return pl.pallas_call(
         clean_kernel,
         grid=(length // width,),
         in_specs=[
-            pl.BlockSpec((channels, 2 * count), lambda i: (0, 0)),
-            pl.BlockSpec((1, channels, width), lambda i: (0, 0, i)),
+            pl.BlockSpec(wide.shape, lambda i: (0, 0)),
+            pl.BlockSpec((1, channels, width), lambda i: (0, 0, i + skip)),
             pl.BlockSpec((count, width), lambda i: (0, i)),
-        ],
-        out_specs=pl.BlockSpec((1, channels, width), lambda i: (0, 0, i)),
+        ]
+        + [pl.BlockSpec(memory_space=pl.ANY)] * len(held),
+        out_specs=pl.BlockSpec((1, channels, width), lambda i: (0, 0, i + skip)),
         out_shape=jax.ShapeDtypeStruct(sky_data.shape, jnp.bfloat16),
+        input_output_aliases={3: 0} if held else {},
+        cost_estimate=pl.CostEstimate(
+            flops=4 * channels * count * length,
+            bytes_accessed=6 * channels * length,
+            transcendentals=0,
+        ),
         compiler_params=pltpu.CompilerParams(vmem_limit_bytes=40 * 2**20),
-    )(wide, sky_data, everyone)
+    )(wide, sky_data, signal, *held)
+
+
+def body(sky_data, eigenmodes, noise_power):
+    channels, length = sky_data.shape[1:]
+    position = lax.axis_index("blk")
+    local_modes = lax.dynamic_slice_in_dim(eigenmodes, position * channels, channels, 0)
+    top, rest = split_rounded(local_modes)
+    wide = jnp.concatenate([top, rest], axis=1)
+    signal = wiener(project(sky_data, local_modes)[None], noise_power)
+    narrow = signal[0].astype(jnp.bfloat16)
+    cut = length // 4 * 3
+    early = lax.all_gather(narrow[:, :cut], "blk", axis=0, tiled=True)
+    late = lax.all_gather(narrow[:, cut:], "blk", axis=0, tiled=True)
+    cleaned = clean(sky_data, wide, early, 0, None)
+    cleaned = clean(sky_data, wide, late, cut, cleaned)
     return (cleaned, signal)
 
 

time: 181 us -> 176 us (0.972)
  waiting for transfers between devices: 43.8 us -> 37.1 us
    all_gather x1 -> x2, waiting for transfers between devices: 43.8 us -> 37.1 us  [the longest x1 34.2 us: body(): early = lax.all_gather(narrow[:, :cut], 'blk', axis=0, tiled=True)]
    pallas_call x1 -> x2, Pallas kernels: 23.4 us -> 24.3 us  [clean(): pl.pallas_call(clean_kernel, grid=(length // width,), in_specs=[pl.BlockS...]
    unnamed x9 -> x11, local copies, waits for them, and re-layouts: 3.27 us -> 3.65 us
  transfers between devices with their start and end apart: 1 -> 2, of which waited for: 1 -> 2; matrix products, arithmetic and copies ran while one was open for 1% -> 1% of each run, Pallas kernels for 0% -> 10%
where the time goes in v3:
time: 176 us
  Pallas kernels  98.6 us (56%)
  waiting for transfers between devices  37.1 us (21%)
  matrix products  14.3 us (8%)
  between operations  14.3 us (8%)
  local copies, waits for them, and re-layouts  9.87 us (6%)
    pallas_call x1, Pallas kernels, project(): pl.pallas_call(functools.partial(scatter_kernel, chips, chunks, wire), gr...  59.9 us
    all_gather x1, waiting for transfers between devices, body(): early = lax.all_gather(narrow[:, :cut], 'blk', axis=0, tiled=True)  34.2 us
    pallas_call x2, Pallas kernels, clean(): pl.pallas_call(clean_kernel, grid=(length // width,), in_specs=[pl.BlockS...  24.3 us
    pallas_call x1, Pallas kernels, sum_over_dishes(): pl.pallas_call(functools.partial(power_kernel, rounds), in_specs=[pl.Bloc...  14.4 us
    unnamed x11, local copies, waits for them, and re-layouts  3.65 us
  transfers between devices with their start and end apart: 2, of which 2 were waited for; matrix products, arithmetic and copies ran while one was open for 1% of the time, Pallas kernels for 10%

profile of v3, /device:TPU:0, one launch (start us, length us, event | category | flops | bytes accessed | tf_op | source)
XLA Modules:
  0.0 175.9 jit_solution(12721219556996321222)
XLA Ops:
  7.2 0.0 copy-start
  7.2 0.0 all-gather.5.cloned.1.call-start
  7.2 0.5 fusion.63
  7.8 0.4 copy-done
  8.2 0.6 maximum_bitcast_fusion.modes_ref
  8.9 59.9 %shard_map.50 = f32[16,16,1024]{2,1,0:T(8,128)} custom-call(bf16[128,256]{1,0:T(8,128)(2,1)} %maximum_bitcast_fusion.modes_ref, f32[1,256,32768]{2,1,0:T(8,128)} %sky_ref.5), custom_call_target="tpu_custom_call" | custom-call | tf_op jit(solution)/shard_map/pallas_call | solution.py:287
  68.8 0.0 copy-start.4
  68.8 2.1 %copy.69 = f32[16,2,8,1024]{3,1,0,2:T(2,128)S(1)} copy(f32[16,2,8,1024]{3,2,1,0:T(8,128)} %bitcast.59) | data formatting | bytes 2097152 | tf_op jit(solution)/shard_map/reshape | solution.py:304
  70.9 0.8 reshape_reshape_broadcast_in_dim_reshape.3
  71.7 1.9 %convolution_negate_fusion = f32[8,128,256]{2,1,0:T(8,128)S(1)} fusion(f32[8,256,128]{2,1,0:T(8,128)S(1)} %reshape_reshape_broadcast_in_dim_reshape.3), kind=kOutput, calls=%fused_computation.9 | convolution fusion | flops 403832832 | bytes 2097152 | tf_op jit(solution)/shard_map/bqp,qk->bpk/dot_general | solution.py:35
  73.6 1.8 %fusion.29 = f32[8,128,256]{2,1,0:T(8,128)S(1)} fusion(f32[8,256,128]{2,1,0:T(8,128)S(1)} %reshape_reshape_broadcast_in_dim_reshape.3), kind=kOutput, calls=%fused_computation.43 | convolution fusion | flops 403570688 | bytes 2097152 | tf_op jit(solution)/shard_map/bqp,qk->bpk/dot_general | solution.py:34
  75.4 0.9 fusion.35
  76.3 0.9 fusion.34
  77.2 0.9 fusion.3
  78.1 1.0 multiply_add_fusion
  79.1 14.4 %shard_map.51 = f32[8,128,256]{2,1,0:T(8,128)S(1)} custom-call(f32[8,128,256]{2,1,0:T(8,128)S(1)} %get-tuple-element.8.here_ref), custom_call_target="tpu_custom_call" | custom-call | tf_op jit(solution)/shard_map/pallas_call | solution.py:345
  93.6 0.0 copy-done.4
  93.6 0.4 add_divide_fusion
  94.0 0.8 fusion.21
  94.8 1.0 fusion.17
  95.9 0.8 fusion
  96.7 0.9 fusion.1
  97.6 1.6 fusion.9
  99.2 1.6 fusion.124
  100.9 0.3 copy.45
  101.2 0.8 slice.9
  102.0 0.0 all-gather.5.cloned.1.call-update
  102.0 0.0 all-gather.3.cloned.1.call-start
  102.1 0.7 slice.8
  102.7 0.0 all-gather.3.cloned.1.call-update
  102.8 0.1 copy.65
  102.9 0.3 copy.46
  103.2 1.2 reshape_reshape.3
  104.4 0.1 pad_maximum_fusion.modes_ref
  104.5 34.2 %all-gather.5.cloned.1.call-done.signal_ref = bf16[64,24576]{1,0:T(8,128)(2,1)} async-done(((bf16[8,24576]{1,0:T(8,128)(2,1)}), bf16[64,24576]{1,0:T(8,128)(2,1)}) %all-gather.5.cloned.1.call-update) | async-done | bytes 3145744 | tf_op jit(solution)/shard_map/all_gather | solution.py:408
  138.7 0.0 copy-start.2
  138.7 1.9 %copy-done.2 = bf16[64,24576]{1,0:T(8,128)(2,1)S(1)} copy-done((bf16[64,24576]{1,0:T(8,128)(2,1)S(1)}, bf16[64,24576]{1,0:T(8,128)(2,1)}, u32[]{:S(2)}) %copy-start.2) | copy-done | bytes 3145752
  140.6 17.8 %shard_map.52.rest_0_ = bf16[1,256,32768]{2,1,0:T(8,128)(2,1)} custom-call(bf16[256,128]{1,0:T(8,128)(2,1)S(1)} %pad_maximum_fusion.modes_ref, f32[1,256,32768]{2,1,0:T(8,128)} %sky_ref.5, bf16[64,24576]{1,0:T(8,128)(2,1)S(1)} %copy-done.2), custom_call_target="tpu_custom_call" | custom-call | flops 1610612736 | bytes 37748736 | tf_op jit(solution)/shard_map/pallas_call | solution.py:378
  158.4 2.9 %all-gather.3.cloned.1.call-done.signal_ref = bf16[64,8192]{1,0:T(8,128)(2,1)} async-done(((bf16[8,8192]{1,0:T(8,128)(2,1)}), bf16[64,8192]{1,0:T(8,128)(2,1)}) %all-gather.3.cloned.1.call-update) | async-done | bytes 1048592 | tf_op jit(solution)/shard_map/all_gather | solution.py:409
  161.3 0.0 copy-start.3
  161.3 1.2 copy-done.3
  162.5 0.0 copy-start.1
  162.5 6.5 %shard_map.53 = bf16[1,256,32768]{2,1,0:T(8,128)(2,1)} custom-call(bf16[256,128]{1,0:T(8,128)(2,1)S(1)} %pad_maximum_fusion.modes_ref, f32[1,256,32768]{2,1,0:T(8,128)} %sky_ref.5, bf16[64,8192]{1,0:T(8,128)(2,1)S(1)} %copy-done.3, bf16[1,256,32768]{2,1,0:T(8,128)(2,1)} %shard_map.52.rest_0_), custom_call_target="tpu_custom_call", output_to_operand_aliasing={{}: (3, {})} | custom-call | flops 536870912 | bytes 12582912 | tf_op jit(solution)/shard_map/pallas_call | solution.py:378
  169.0 0.0 copy-done.1
  (4 shorter events, 0.0 us)
Async XLA Ops:
  7.2 1.1 copy-start
  7.2 131.5 %all-gather.5.cloned.1.call-start = ((), (), s32[]{:S(2)}) async-start(), calls=%async_computation.1 | async-start | bytes 3538944 | tf_op jit(solution)/shard_map/all_gather | solution.py:408
  68.8 24.8 %copy-start.4 = (f32[8,32768]{1,0:T(8,128)S(1)}, f32[8,32768]{1,0:T(8,128)}, u32[]{:S(2)}) copy-start(f32[8,32768]{1,0:T(8,128)} %param.5) | copy-start | bytes 3145732
  102.0 59.3 %all-gather.3.cloned.1.call-start = ((), (), s32[]{:S(2)}) async-start(), calls=%async_computation | async-start | bytes 1179648 | tf_op jit(solution)/shard_map/all_gather | solution.py:409
  138.7 1.9 %copy-start.2 = (bf16[64,24576]{1,0:T(8,128)(2,1)S(1)}, bf16[64,24576]{1,0:T(8,128)(2,1)}, u32[]{:S(2)}) copy-start(bf16[64,24576]{1,0:T(8,128)(2,1)} %all-gather.5.cloned.1.call-done.signal_ref) | copy-start | bytes 9437188
  161.3 1.2 copy-start.3
  162.5 6.5 %copy-start.1 = (f32[2048,64]{0,1:T(8,128)S(1)}, f32[2048,64]{0,1:T(8,128)}, u32[]{:S(2)}) copy-start(f32[2048,64]{0,1:T(8,128)} %param.4) | copy-start | bytes 1572868
Sparse Core Ops, SparseCore 0:
  102.1 36.5 all-gather.4
  140.3 20.9 all-gather.2
